TPU v7x, 256 devices: a whole 4x4x8 slice. The times are simulated.
256 devices in a mesh: row: 32 (over z_lo, y, x), col: 8 (over z_hi, core).
Axes of the slice: x: 4, y: 4, z: 8 (z_hi: 4, z_lo: 2; z = z_hi * 2 + z_lo), core: 2. Of those that a mesh axis runs over, the one named last changes fastest.
Arguments:
- features: bfloat16 [512, 512, 1024], P('row', None, 'col'), may hold values from -6 to 6
- projection: bfloat16 [512, 4], replicated, may hold values from -0.25 to 0.25
- norm_gain: bfloat16 [2048], replicated, may hold values from 0.25 to 1.75
- norm_shift: bfloat16 [2048], replicated, may hold values from -6 to 6
- weight_in: bfloat16 [2048, 4096], P(None, 'col'), may hold values from -0.125 to 0.125
- weight_out: bfloat16 [4096, 1, 1024], P('col'), may hold values from -0.09375 to 0.09375
- cotangent: bfloat16 [512, 1, 1024], P('row', None, 'col'), may hold values from -6 to 6
Outputs:
- mixed: bfloat16 [512, 1, 1024], P('row', None, 'col')
- grad_features: bfloat16 [512, 512, 1024], P('row', None, 'col')
- grad_gain: float32 [2048], replicated
- grad_shift: float32 [2048], replicated
- grad_weight_in: bfloat16 [2048, 4096], P(None, 'col')
- grad_weight_out: bfloat16 [4096, 1, 1024], P('col')
All inputs are finite; a program needn't handle non-finite values.
Results may differ from a plain program's by a relative error of at most 0.013.
Values may be sent and summed in bfloat16 or wider, within the bound.
A program may use at most 64 MiB of HBM per device.

v0:
```python
import jax
import jax.numpy as jnp
from jax import lax
from jax.sharding import PartitionSpec as P


def layer_norm(inter, norm_gain, norm_shift):
    mean = jnp.mean(inter, axis=1, keepdims=True)
    centered = inter - mean
    rstd = lax.rsqrt(jnp.mean(centered * centered, axis=1, keepdims=True) + 1e-05)
    unit = centered * rstd
    normed = (unit * norm_gain.astype(jnp.float32) + norm_shift.astype(jnp.float32)).astype(
        jnp.bfloat16
    )
    return (normed, unit, rstd)


def on_device(features, projection, norm_gain, norm_shift, weight_in, weight_out, cotangent):
    batch = features.shape[0]
    embeds = features.shape[1]
    reduced = jnp.einsum(
        "bnd,nk->bdk", features, projection, preferred_element_type=jnp.float32
    ).astype(jnp.bfloat16)
    partial_inter = jnp.einsum(
        "bnd,bdk->bnk", features, reduced, preferred_element_type=jnp.float32
    ).reshape(batch, -1)
    inter = lax.psum(partial_inter, "col")
    normed, unit, rstd = layer_norm(inter, norm_gain, norm_shift)
    pre = jnp.dot(normed, weight_in, preferred_element_type=jnp.float32)
    act = jax.nn.silu(pre).astype(jnp.bfloat16)
    out_terms = jnp.einsum("bh,hfd->bfd", act, weight_out, preferred_element_type=jnp.float32)
    mixed = lax.psum_scatter(out_terms, "col", scatter_dimension=2, tiled=True).astype(jnp.bfloat16)
    full_grads = lax.all_gather(cotangent, "col", axis=2, tiled=True)
    dact = jnp.einsum("bfd,hfd->bh", full_grads, weight_out, preferred_element_type=jnp.float32)
    sigma = jax.nn.sigmoid(pre)
    dpre = (dact * sigma * (1.0 + pre * (1.0 - sigma))).astype(jnp.bfloat16)
    partial_dnormed = jnp.einsum("bh,ih->bi", dpre, weight_in, preferred_element_type=jnp.float32)
    dnormed = lax.psum(partial_dnormed, "col")
    gain_terms = jnp.sum(dnormed * unit, axis=0)
    shift_terms = jnp.sum(dnormed, axis=0)
    in_terms = jnp.einsum("bi,bh->ih", normed, dpre, preferred_element_type=jnp.float32)
    out_grad_terms = jnp.einsum("bh,bfd->hfd", act, full_grads, preferred_element_type=jnp.float32)
    grad_in, grad_out, grad_gain, grad_shift = lax.psum(
        (in_terms, out_grad_terms, gain_terms, shift_terms), "row"
    )
    scaled = dnormed * norm_gain.astype(jnp.float32)
    dinter = rstd * (
        scaled
        - jnp.mean(scaled, axis=1, keepdims=True)
        - unit * jnp.mean(scaled * unit, axis=1, keepdims=True)
    )
    dinter = dinter.reshape(batch, embeds, -1)
    dreduced = jnp.einsum("bnd,bnk->bdk", features, dinter, preferred_element_type=jnp.float32)
    grad_features = jnp.einsum("bnk,bdk->bnd", dinter, reduced, preferred_element_type=jnp.float32)
    grad_features = grad_features + jnp.einsum(
        "nk,bdk->bnd", projection, dreduced, preferred_element_type=jnp.float32
    )
    return (
        mixed,
        grad_features.astype(jnp.bfloat16),
        grad_gain,
        grad_shift,
        grad_in.astype(jnp.bfloat16),
        grad_out.astype(jnp.bfloat16),
    )


def solution(mesh):
    placed = (
        P("row", None, "col"),
        P(),
        P(),
        P(),
        P(None, "col"),
        P("col", None, None),
        P("row", None, "col"),
    )
    return jax.shard_map(
        on_device,
        mesh=mesh,
        in_specs=placed,
        out_specs=(
            P("row", None, "col"),
            P("row", None, "col"),
            P(),
            P(),
            P(None, "col"),
            P("col", None, None),
        ),
        check_vma=False,
    )
```

profile of v0, /device:TPU:32, one launch (start us, length us, event | category | flops | bytes accessed | tf_op | source)
XLA Modules:
  0.0 379.2 jit_solution(18031466390064069782)
XLA Ops:
  7.2 0.0 copy-start
  7.2 0.0 all-reduce.5.cloned.1.call-start
  7.2 1.5 copy-done
  8.8 1.1 convolution_convert_fusion
  9.8 0.0 copy-start.5
  9.8 0.0 copy-start.6
  9.8 0.0 copy-start.7
  9.8 0.6 convolution_bitcast_fusion.1
  10.5 0.4 copy.15
  10.9 1.0 copy.16
  11.9 0.0 all-reduce.5.cloned.1.call-update
  11.9 0.0 all-reduce.7.cloned.1.call-start
  11.9 0.0 copy-done.5
  12.0 0.0 copy-done.6
  12.0 0.0 copy-done.7
  12.0 17.3 %all_gather.3 = bf16[16,1,1024]{2,0,1:T(8,128)(2,1)S(1)} all-gather(bf16[16,1,128]{2,0,1:T(8,128)(2,1)S(1)} %copy-done.7), channel_id=1, replica_groups=mesh['row'=32,'col'=8] {'col'}, dimensions={2}, use_global_device_ids=true | all-gather | bytes 36864 | tf_op jit(solution)/shard_map/all_gather | solution.py:33
  29.3 56.6 %all-reduce.5.cloned.1.call-done = f32[16,2048]{1,0:T(8,128)} async-done(((f32[16,2048]{1,0:T(8,128)}), f32[16,2048]{1,0:T(8,128)}) %all-reduce.5.cloned.1.call-update) | async-done | bytes 131088 | tf_op jit(solution)/shard_map/psum | solution.py:27
  85.8 1.0 reduce_sum.54
  86.9 1.1 multiply_reduce_fusion.2
  88.0 0.0 copy-start.3
  88.0 2.2 fusion.10
  90.2 0.0 copy-start.1
  90.2 1.9 convolution_bitcast_fusion
  92.0 0.0 copy-done.3
  92.0 0.0 copy-start.2
  92.0 0.4 fusion.2
  92.4 0.0 copy-done.1
  92.4 1.3 fusion.11
  93.8 0.0 all-reduce.7.cloned.1.call-update
  93.8 0.0 reduce-scatter.2.cloned.1.call-start
  93.8 0.0 copy-done.2
  93.8 2.7 fusion.9
  96.6 0.9 convolution_bitcast_fusion.2
  97.4 0.0 reduce-scatter.2.cloned.1.call-update
  97.5 66.6 %all-reduce.7.cloned.1.call-done = f32[16,2048]{1,0:T(8,128)} async-done(((f32[16,2048]{1,0:T(8,128)}), f32[16,2048]{1,0:T(8,128)}) %all-reduce.7.cloned.1.call-update) | async-done | bytes 131088 | tf_op jit(solution)/shard_map/psum | solution.py:38
  164.1 1.1 multiply_reduce_fusion
  165.2 1.0 subtract_multiply_fusion
  166.2 0.3 copy.17
  166.5 0.3 copy.18
  166.8 0.0 copy-start.4
  166.9 2.8 fusion.12
  169.6 0.0 copy-done.4
  169.6 4.5 %fusion = bf16[16,512,128]{2,1,0:T(8,128)(2,1)} fusion(f32[16,512,128]{2,1,0:T(8,128)} %fusion.12, bf16[16,512,4]{1,2,0:T(4,128)(2,1)S(1)} %copy.18, bf16[16,512,128]{2,1,0:T(8,128)(2,1)S(1)} %copy-done, bf16[512,4]{0,1:T(4,128)(2,1)S(1)} %copy-done.4), kind=kOutput, calls=%fused_computation.1 | convolution fusion | flops 18874368 | bytes 8458240 | tf_op jit(solution)/shard_map/nk,bdk->bnd/dot_general | solution.py:55
  174.1 197.3 %all-reduce.8 = (f32[2048]{0:T(1024)}, f32[2048]{0:T(1024)}, bf16[2048,512]{1,0:T(8,128)(2,1)}, bf16[512,1,1024]{2,0,1:T(8,128)(2,1)}) all-reduce(f32[2048]{0:T(1024)S(1)} %get-tuple-element.6, f32[2048]{0:T(1024)S(1)} %get-tuple-element.9, f32[2048,512]{1,0:T(8,128)} %fusion.9, ...), channel_id=1, replica_groups=mesh['row'=32,'col'=8] {'row'}, use_global_device_ids=true, to_apply=%region_8.9 | all-reduce | flops 1576960 | bytes 9469952 | tf_op jit(solution)/shard_map/psum | solution.py:43
  371.3 0.0 reduce-scatter.2.cloned.1.call-done
  371.3 1.3 convert_element_type.36
  (5 shorter events, 0.0 us)
Async XLA Ops:
  7.2 1.6 copy-start
  7.2 78.6 %all-reduce.5.cloned.1.call-start = ((), (), s32[]{:S(2)}) async-start(), calls=%async_computation.1 | async-start | bytes 262144 | tf_op jit(solution)/shard_map/psum | solution.py:27
  9.8 2.1 copy-start.5
  9.8 2.1 copy-start.6
  9.8 2.2 copy-start.7
  11.9 152.2 %all-reduce.7.cloned.1.call-start = ((), (), s32[]{:S(2)}) async-start(), calls=%async_computation.3 | async-start | bytes 262144 | tf_op jit(solution)/shard_map/psum | solution.py:38
  88.0 4.1 %copy-start.3 = (bf16[512,1,1024]{2,0,1:T(8,128)(2,1)S(1)}, bf16[512,1,1024]{2,0,1:T(8,128)(2,1)}, u32[]{:S(2)}) copy-start(bf16[512,1,1024]{2,0,1:T(8,128)(2,1)} %param.12) | copy-start | bytes 3145732
  90.2 2.3 copy-start.1
  92.0 1.8 copy-start.2
  93.8 277.6 %reduce-scatter.2.cloned.1.call-start = ((), (), s32[]{:S(2)}) async-start(), calls=%async_computation.2 | async-start | bytes 73728 | tf_op jit(solution)/shard_map/reduce_scatter | solution.py:32
  166.8 2.8 copy-start.4
Sparse Core Ops, SparseCore 0:
  12.0 73.7 all-reduce.4
  93.9 70.1 all-reduce.6
  166.6 35.4 reduce-scatter.1
where the time goes:
time: 380 us; the launch traced here: 379 us
  blocking collectives  215 us (57%)
  waiting for transfers between devices  123 us (32%)
  matrix products  18.3 us (5%)
  between operations  13.9 us (4%)
  other arithmetic  5.58 us (1%)
    psum x1, blocking collectives, on_device(): lax.psum((in_terms, out_grad_terms, gain_terms, shift_terms), 'row')  197 us
    psum x1, waiting for transfers between devices, on_device(): dnormed = lax.psum(partial_dnormed, 'col')  66.6 us
    psum x1, waiting for transfers between devices, on_device(): inter = lax.psum(partial_inter, 'col')  56.6 us
    all_gather x1, blocking collectives, on_device(): full_grads = lax.all_gather(cotangent, 'col', axis=2, tiled=True)  17.3 us
  transfers between devices with their start and end apart: 3, of which 2 were waited for; matrix products, arithmetic and copies ran while one was open for 4% of the time, Pallas kernels for 0%

commit v1 on v0

--- a/solution.py
+++ b/solution.py
@@ -2,6 +2,12 @@
 import jax.numpy as jnp
 from jax import lax
 from jax.sharding import PartitionSpec as P
+
+
+def gather_and_add(shard, mesh_axis):
+    parts = lax.all_gather(shard, mesh_axis, axis=0, tiled=False)
+    total = parts.sum(axis=0)
+    return total
 
 
 def layer_norm(inter, norm_gain, norm_shift):
@@ -24,7 +30,7 @@
     partial_inter = jnp.einsum(
         "bnd,bdk->bnk", features, reduced, preferred_element_type=jnp.float32
     ).reshape(batch, -1)
-    inter = lax.psum(partial_inter, "col")
+    inter = gather_and_add(partial_inter, "col")
     normed, unit, rstd = layer_norm(inter, norm_gain, norm_shift)
     pre = jnp.dot(normed, weight_in, preferred_element_type=jnp.float32)
     act = jax.nn.silu(pre).astype(jnp.bfloat16)

time: 380 us -> 340 us (0.89)
  waiting for transfers between devices: 123 us -> 84.3 us
    psum x1 -> x0, waiting for transfers between devices: 56.6 us -> none  [on_device(): inter = lax.psum(partial_inter, 'col')]
    all_gather x0 -> x1, waiting for transfers between devices: none -> 14.3 us  [gather_and_add(): parts = lax.all_gather(shard, mesh_axis, axis=0, tiled=False)]
  transfers between devices with their start and end apart: 3 -> 3, of which waited for: 2 -> 2; matrix products, arithmetic and copies ran while one was open for 4% -> 3% of each run, Pallas kernels for 0% -> 0%
where the time goes in v1:
time: 340 us
  blocking collectives  215 us (63%)
  waiting for transfers between devices  84.3 us (25%)
  matrix products  18.2 us (5%)
  between operations  13.9 us (4%)
  other arithmetic  5.14 us (2%)
  local copies, waits for them, and re-layouts  3.53 us (1%)
    psum x1, blocking collectives, on_device(): lax.psum((in_terms, out_grad_terms, gain_terms, shift_terms), 'row')  198 us
    psum x1, waiting for transfers between devices, on_device(): dnormed = lax.psum(partial_dnormed, 'col')  69.9 us
    all_gather x1, blocking collectives, on_device(): full_grads = lax.all_gather(cotangent, 'col', axis=2, tiled=True)  17.3 us
    all_gather x1, waiting for transfers between devices, gather_and_add(): parts = lax.all_gather(shard, mesh_axis, axis=0, tiled=False)  14.3 us
  transfers between devices with their start and end apart: 3, of which 2 were waited for; matrix products, arithmetic and copies ran while one was open for 3% of the time, Pallas kernels for 0%

profile of v1, /device:TPU:32, one launch (start us, length us, event | category | flops | bytes accessed | tf_op | source)
XLA Modules:
  0.0 340.1 jit_solution(1303184620530049699)
XLA Ops:
  7.2 0.0 copy-start
  7.2 0.0 all-gather.2.cloned.1.call-start
  7.2 1.5 copy-done
  8.8 1.1 convolution_convert_fusion
  9.8 0.0 copy-start.4
  9.8 0.0 copy-start.5
  9.8 0.0 copy-start.6
  9.8 0.6 convolution_bitcast_fusion.1
  10.5 0.4 copy.19
  10.9 1.0 copy.20
  11.9 0.0 all-gather.2.cloned.1.call-update
  11.9 0.0 all-reduce.4.cloned.1.call-start
  11.9 0.0 copy-done.4
  12.0 0.0 copy-done.5
  12.0 0.0 copy-done.6
  12.0 17.3 %all_gather.7 = bf16[16,1,1024]{2,0,1:T(8,128)(2,1)S(1)} all-gather(bf16[16,1,128]{2,0,1:T(8,128)(2,1)S(1)} %copy-done.6), channel_id=1, replica_groups=mesh['row'=32,'col'=8] {'col'}, dimensions={2}, use_global_device_ids=true | all-gather | bytes 36864 | tf_op jit(solution)/shard_map/all_gather | solution.py:39
  29.3 14.3 %all-gather.2.cloned.1.call-done = f32[8,16,2048]{2,1,0:T(8,128)} async-done(((f32[1,16,2048]{2,1,0:T(8,128)}), f32[8,16,2048]{2,1,0:T(8,128)}) %all-gather.2.cloned.1.call-update) | async-done | bytes 1048592 | tf_op jit(solution)/shard_map/all_gather | solution.py:8
  43.6 1.5 fusion.11
  45.1 0.2 multiply_reduce_fusion.2
  45.3 0.0 copy-start.2
  45.3 2.1 fusion.10
  47.4 0.0 copy-start.1
  47.4 1.9 convolution_bitcast_fusion
  49.3 0.0 copy-done.2
  49.3 0.4 fusion.2
  49.6 0.0 copy-done.1
  49.6 1.3 fusion.12
  51.0 2.7 fusion.9
  53.7 0.0 all-reduce.4.cloned.1.call-update
  53.7 0.0 reduce-scatter.2.cloned.1.call-start
  53.8 0.9 convolution_bitcast_fusion.2
  54.7 0.0 reduce-scatter.2.cloned.1.call-update
  54.7 69.9 %all-reduce.4.cloned.1.call-done = f32[16,2048]{1,0:T(8,128)} async-done(((f32[16,2048]{1,0:T(8,128)}), f32[16,2048]{1,0:T(8,128)}) %all-reduce.4.cloned.1.call-update) | async-done | bytes 131088 | tf_op jit(solution)/shard_map/psum | solution.py:44
  124.6 1.1 multiply_reduce_fusion
  125.8 1.0 subtract_multiply_fusion
  126.8 0.3 copy.23
  127.0 0.3 copy.24
  127.4 0.0 copy-start.3
  127.4 2.8 fusion.13
  130.1 0.0 copy-done.3
  130.1 4.5 %fusion = bf16[16,512,128]{2,1,0:T(8,128)(2,1)} fusion(f32[16,512,128]{2,1,0:T(8,128)} %fusion.13, bf16[16,512,4]{1,2,0:T(4,128)(2,1)S(1)} %copy.24, bf16[16,512,128]{2,1,0:T(8,128)(2,1)S(1)} %copy-done, bf16[512,4]{0,1:T(4,128)(2,1)S(1)} %copy-done.3), kind=kOutput, calls=%fused_computation.1 | convolution fusion | flops 18874368 | bytes 8458240 | tf_op jit(solution)/shard_map/nk,bdk->bnd/dot_general | solution.py:61
  134.6 197.7 %all-reduce.5 = (f32[2048]{0:T(1024)}, f32[2048]{0:T(1024)}, bf16[2048,512]{1,0:T(8,128)(2,1)}, bf16[512,1,1024]{2,0,1:T(8,128)(2,1)}) all-reduce(f32[2048]{0:T(1024)S(1)} %get-tuple-element.8, f32[2048]{0:T(1024)S(1)} %get-tuple-element.11, f32[2048,512]{1,0:T(8,128)} %fusion.9, ...), channel_id=1, replica_groups=mesh['row'=32,'col'=8] {'row'}, use_global_device_ids=true, to_apply=%region_8.9 | all-reduce | flops 1576960 | bytes 9469952 | tf_op jit(solution)/shard_map/psum | solution.py:49
  332.3 0.0 reduce-scatter.2.cloned.1.call-done
  332.3 1.3 convert_element_type.36
  (5 shorter events, 0.0 us)
Async XLA Ops:
  7.2 1.6 copy-start
  7.2 36.4 %all-gather.2.cloned.1.call-start = ((), (), s32[]{:S(2)}) async-start(), calls=%async_computation.1 | async-start | bytes 1179648 | tf_op jit(solution)/shard_map/all_gather | solution.py:8
  9.8 2.1 copy-start.4
  9.8 2.1 copy-start.5
  9.8 2.2 copy-start.6
  11.9 112.7 %all-reduce.4.cloned.1.call-start = ((), (), s32[]{:S(2)}) async-start(), calls=%async_computation.3 | async-start | bytes 262144 | tf_op jit(solution)/shard_map/psum | solution.py:44
  45.3 4.0 %copy-start.2 = (bf16[512,1,1024]{2,0,1:T(8,128)(2,1)S(1)}, bf16[512,1,1024]{2,0,1:T(8,128)(2,1)}, u32[]{:S(2)}) copy-start(bf16[512,1,1024]{2,0,1:T(8,128)(2,1)} %param.12) | copy-start | bytes 3145732
  47.4 2.3 copy-start.1
  53.7 278.5 %reduce-scatter.2.cloned.1.call-start = ((), (), s32[]{:S(2)}) async-start(), calls=%async_computation.2 | async-start | bytes 73728 | tf_op jit(solution)/shard_map/reduce_scatter | solution.py:38
  127.4 2.8 copy-start.3
Sparse Core Ops, SparseCore 0:
  12.0 31.5 all-gather.1
  53.9 70.7 all-reduce.3
  127.3 35.4 reduce-scatter.1
